TPU v7x, 32 devices: a whole 2x2x4 slice. The times are simulated.
32 devices in a mesh: dp: 8 (over z, y), rows: 4 (over x, core).
Axes of the slice: x: 2, y: 2, z: 4, core: 2. Of those that a mesh axis runs over, the one named last changes fastest.
Arguments:
- images: bfloat16 [8, 48, 64, 256], P('dp', 'rows'), may hold values from -6 to 6
- kernel: bfloat16 [3, 3, 256, 256], replicated, may hold values from -0.125 to 0.125
- cotangent: bfloat16 [8, 48, 64, 256], P('dp', 'rows'), may hold values from -6 to 6
Outputs:
- output_maps: bfloat16 [8, 48, 64, 256], P('dp', 'rows')
- grad_input: bfloat16 [8, 48, 64, 256], P('dp', 'rows')
- grad_kernel: float32 [3, 3, 256, 256], P(None, None, None, 'rows')
All inputs are finite; a program needn't handle non-finite values.
Results may differ from a plain program's by a relative error of at most 0.001.
Values may be sent and summed in bfloat16 or wider, within the bound.
A program may use at most 64 MiB of HBM per device.

v0:
```python
import jax
import jax.numpy as jnp
from jax import lax
from jax.sharding import PartitionSpec as P


def padded_2(x, sides, width):
    for axis, dim in sides:
        size, length = (lax.axis_size(axis), x.shape[dim])
        up = [(i, (i + 1) % size) for i in range(size - 1)]
        down = [(j, i) for i, j in up]
        last = lax.slice_in_dim(x, length - width, length, axis=dim)
        initial = lax.slice_in_dim(x, 0, width, axis=dim)
        before = lax.ppermute(last, axis, up)
        after = lax.ppermute(initial, axis, down)
        x = jnp.concatenate([before, x, after], axis=dim)
    return x


def conv_rows(inputs, weights):
    return lax.conv_general_dilated(
        inputs,
        weights,
        (1, 1),
        ((0, 0), (1, 1)),
        dimension_numbers=("NHWC", "HWIO", "NHWC"),
        preferred_element_type=jnp.float32,
    )


def shards(images, kernel, cotangent):
    rows_dev = images.shape[1]
    columns = images.shape[2]
    wide_images = padded_2(images, (("rows", 1),), 1)
    wide_grads = padded_2(cotangent, (("rows", 1),), 1)
    flipped = jnp.transpose(kernel[::-1, ::-1], (0, 1, 3, 2))
    output_maps = conv_rows(wide_images, kernel).astype(jnp.bfloat16)
    grad_input = conv_rows(wide_grads, flipped).astype(jnp.bfloat16)
    padded = jnp.pad(wide_images, ((0, 0), (0, 0), (1, 1), (0, 0)))
    tap_rows = []
    for tap_row in range(3):
        tap_line = []
        for tap_col in range(3):
            window = padded[:, tap_row : tap_row + rows_dev, tap_col : tap_col + columns]
            tap_line.append(
                jnp.einsum("bhwc,bhwd->cd", window, cotangent, preferred_element_type=jnp.float32)
            )
        tap_rows.append(jnp.stack(tap_line))
    local_terms = jnp.stack(tap_rows)
    groups = lax.axis_size("dp")
    row_share = lax.psum_scatter(local_terms, "rows", scatter_dimension=3, tiled=True)
    summed = lax.psum(row_share, "dp")
    batch_total = images.shape[0] * groups
    return (output_maps, grad_input, summed / float(batch_total))


def solution(mesh):
    return jax.shard_map(
        shards,
        mesh=mesh,
        in_specs=(P("dp", "rows", None, None), P(), P("dp", "rows", None, None)),
        out_specs=(
            P("dp", "rows", None, None),
            P("dp", "rows", None, None),
            P(None, None, None, "rows"),
        ),
        check_vma=False,
    )
```

profile of v0, /device:TPU:0, one launch (start us, length us, event | category | flops | bytes accessed | tf_op | source)
XLA Modules:
  0.0 180.4 jit_solution(7106152800115837669)
XLA Ops:
  7.2 0.0 copy-start
  7.2 0.0 copy-start.3
  7.2 0.0 copy-start.1
  7.2 0.0 all-reduce.7.cloned.1.call-start
  7.2 0.9 fusion.67
  8.2 2.3 %collective-permute-start = (bf16[1,1,64,256]{3,2,1,0:T(8,128)(2,1)S(1)}, bf16[1,1,64,256]{3,2,1,0:T(8,128)(2,1)S(1)}, u32[]{:S(2)}, u32[]{:S(2)}) collective-permute-start(bf16[1,1,64,256]{3,2,1,0:T(8,128)(2,1)S(1)} %get-tuple-element.15), channel_id=1, source_target_pairs={{0,1},{1,2},{2,3},{4,5},{5,6},{6,7},{8,9},{9,10},{10,11},{12,13},{... | collective-permute-start | bytes 98312 | tf_op jit(solution)/shard_map/ppermute | solution.py:14
  10.5 1.3 collective-permute-start.1
  11.8 1.4 convolution_bitcast_fusion.4
  13.2 0.0 collective-permute-done
  13.3 0.0 copy-done.3
  13.3 2.4 %collective-permute-done.1 = bf16[1,1,64,256]{3,2,1,0:T(8,128)(2,1)S(1)} collective-permute-done((bf16[1,1,64,256]{3,2,1,0:T(8,128)(2,1)S(1)}, bf16[1,1,64,256]{3,2,1,0:T(8,128)(2,1)S(1)}, u32[]{:S(2)}, u32[]{:S(2)}) %collective-permute-start.1) | collective-permute-done | bytes 32800 | tf_op jit(solution)/shard_map/ppermute | solution.py:15
  15.7 0.0 copy-done.1
  15.7 0.0 copy-start.4
  15.7 0.3 convolution_bitcast_fusion.3
  16.0 0.3 convolution_bitcast_fusion.5
  16.4 0.3 convolution_bitcast_fusion.6
  16.7 0.3 convolution_bitcast_fusion.8
  17.0 0.3 convolution_bitcast_fusion
  17.3 0.0 copy-done.4
  17.3 0.3 convolution_bitcast_fusion.2
  17.6 0.3 convolution_bitcast_fusion.1
  17.9 0.1 maximum_bitcast_fusion.2
  18.0 0.3 convolution_bitcast_fusion.7
  18.3 0.1 maximum_bitcast_fusion
  18.4 0.2 pad_maximum_fusion
  18.6 2.9 %copy.26 = f32[3,3,256,256]{2,1,0,3:T(4,128)} copy(f32[3,3,256,256]{3,2,1,0:T(8,128)S(1)} %pad_maximum_fusion) | data formatting | bytes 4718592 | tf_op jit(solution)/shard_map/stack | solution.py:49
  21.5 0.0 copy-start.2
  21.5 0.0 copy-start.6
  21.5 0.0 copy-start.5
  21.5 0.0 all-reduce.7.cloned.1.call-update
  21.5 0.0 all-reduce.5.cloned.1.call-start
  21.6 0.9 copy-done.2
  22.5 4.5 %collective-permute-start.2 = (bf16[1,1,64,256]{3,2,1,0:T(8,128)(2,1)S(1)}, bf16[1,1,64,256]{3,2,1,0:T(8,128)(2,1)S(1)}, u32[]{:S(2)}, u32[]{:S(2)}) collective-permute-start(bf16[1,1,64,256]{3,2,1,0:T(8,128)(2,1)S(1)} %get-tuple-element.12), channel_id=1, source_target_pairs={{0,1},{1,2},{2,3},{4,5},{5,6},{6,7},{8,9},{9,10},{10,11},{12,13},{... | collective-permute-start | bytes 98312 | tf_op jit(solution)/shard_map/ppermute | solution.py:14
  27.0 1.3 collective-permute-start.3
  28.3 0.0 copy-done.6
  28.3 0.6 dynamic-slice
  29.6 0.0 copy-done.5
  29.6 0.3 copy.30
  29.9 0.0 copy-start.7
  29.9 0.1 pad.5.clone
  29.9 0.2 copy.20
  30.1 0.0 copy-done
  30.1 0.4 copy-done.7
  30.6 1.2 fusion
  31.8 0.1 copy.21
  31.9 61.2 %all-reduce.7.cloned.1.call-done = f32[3,3,256,256]{2,1,0,3:T(4,128)} async-done(((f32[3,3,256,256]{2,1,0,3:T(4,128)}), f32[3,3,256,256]{2,1,0,3:T(4,128)}) %all-reduce.7.cloned.1.call-update) | async-done | bytes 2359312
  93.1 2.2 %constant_dynamic-slice_fusion = f32[3,3,256,64]{2,1,0,3:T(4,128)} fusion(f32[3,3,256,256]{2,1,0,3:T(4,128)} %all-reduce.7.cloned.1.call-done, u32[]{:T(128)S(6)} %multiply.2), kind=kLoop, calls=%fused_computation.73 | loop fusion | bytes 1179652
  95.2 0.0 all-reduce.5.cloned.1.call-update
  95.3 0.0 collective-permute-done.2
  95.3 0.0 collective-permute-done.3
  95.3 0.1 maximum_bitcast_fusion.3
  95.4 0.9 copy.27
  96.2 0.3 copy.31
  96.5 0.1 pad.7.clone
  96.5 0.2 copy.24
  96.8 1.2 fusion.1
  98.0 0.1 copy.25
  98.2 0.9 copy.28
  99.0 72.3 %all-reduce.5.cloned.1.call-done = f32[3,3,256,64]{2,1,0,3:T(4,128)} async-done(((f32[3,3,256,64]{2,1,0,3:T(4,128)}), f32[3,3,256,64]{2,1,0,3:T(4,128)}) %all-reduce.5.cloned.1.call-update) | async-done | bytes 589840 | tf_op jit(solution)/shard_map/psum | solution.py:52
  171.3 1.3 broadcast_multiply_fusion
  172.6 0.9 copy.29
  (8 shorter events, 0.2 us)
Async XLA Ops:
  7.2 23.0 %copy-start = (bf16[3,3,256,256]{3,2,1,0:T(8,128)(2,1)S(1)}, bf16[3,3,256,256]{3,2,1,0:T(8,128)(2,1)}, u32[]{:S(2)}) copy-start(bf16[3,3,256,256]{3,2,1,0:T(8,128)(2,1)} %param.4) | copy-start | bytes 3538948
  7.2 6.1 %copy-start.3 = (bf16[1,12,64,256]{3,2,1,0:T(8,128)(2,1)S(1)}, bf16[1,12,64,256]{3,2,1,0:T(8,128)(2,1)}, u32[]{:S(2)}) copy-start(bf16[1,12,64,256]{3,2,1,0:T(8,128)(2,1)} %param.3) | copy-start | bytes 1179652
  7.2 8.5 %copy-start.1 = (bf16[1,12,64,256]{3,2,1,0:T(8,128)(2,1)S(1)}, bf16[1,12,64,256]{3,2,1,0:T(8,128)(2,1)}, u32[]{:S(2)}) copy-start(bf16[1,12,64,256]{3,2,1,0:T(8,128)(2,1)} %param.5) | copy-start | bytes 1179652
  7.2 85.9 %all-reduce.7.cloned.1.call-start = ((), (), s32[]{:S(2)}) async-start(), calls=%async_computation.1 | async-start | bytes 6291456
  8.2 5.1 %collective-permute-start = (bf16[1,1,64,256]{3,2,1,0:T(8,128)(2,1)S(1)}, bf16[1,1,64,256]{3,2,1,0:T(8,128)(2,1)S(1)}, u32[]{:S(2)}, u32[]{:S(2)}) collective-permute-start(bf16[1,1,64,256]{3,2,1,0:T(8,128)(2,1)S(1)} %get-tuple-element.15), channel_id=1, source_target_pairs={{0,1},{1,2},{2,3},{4,5},{5,6},{6,7},{8,9},{9,10},{10,11},{12,13},{... | collective-permute-start | bytes 98312 | tf_op jit(solution)/shard_map/ppermute | solution.py:14
  10.5 5.2 %collective-permute-start.1 = (bf16[1,1,64,256]{3,2,1,0:T(8,128)(2,1)S(1)}, bf16[1,1,64,256]{3,2,1,0:T(8,128)(2,1)S(1)}, u32[]{:S(2)}, u32[]{:S(2)}) collective-permute-start(bf16[1,1,64,256]{3,2,1,0:T(8,128)(2,1)S(1)} %get-tuple-element.14), channel_id=1, source_target_pairs={{1,0},{2,1},{3,2},{5,4},{6,5},{7,6},{9,8},{10,9},{11,10},{13,12},{... | collective-permute-start | bytes 98312 | tf_op jit(solution)/shard_map/ppermute | solution.py:15
  15.7 1.6 copy-start.4
  21.5 1.0 copy-start.2
  21.5 6.8 %copy-start.6 = (u32[32]{0:T(128)S(1)}, u32[32]{0:T(128)}, u32[]{:S(2)}) copy-start(u32[32]{0:T(128)} %constant.22) | copy-start | bytes 388
  21.5 8.1 %copy-start.5 = (bf16[1,14,64,256]{3,2,1,0:T(8,128)(2,1)S(1)}, bf16[1,14,64,256]{3,2,1,0:T(8,128)(2,1)}, u32[]{:S(2)}) copy-start(bf16[1,14,64,256]{3,2,1,0:T(8,128)(2,1)} %copy-done.4) | copy-start | bytes 1376260
  21.5 149.8 %all-reduce.5.cloned.1.call-start = ((), (), s32[]{:S(2)}) async-start(), calls=%async_computation | async-start | bytes 1572864 | tf_op jit(solution)/shard_map/psum | solution.py:52
  22.5 72.8 %collective-permute-start.2 = (bf16[1,1,64,256]{3,2,1,0:T(8,128)(2,1)S(1)}, bf16[1,1,64,256]{3,2,1,0:T(8,128)(2,1)S(1)}, u32[]{:S(2)}, u32[]{:S(2)}) collective-permute-start(bf16[1,1,64,256]{3,2,1,0:T(8,128)(2,1)S(1)} %get-tuple-element.12), channel_id=1, source_target_pairs={{0,1},{1,2},{2,3},{4,5},{5,6},{6,7},{8,9},{9,10},{10,11},{12,13},{... | collective-permute-start | bytes 98312 | tf_op jit(solution)/shard_map/ppermute | solution.py:14
  27.0 68.3 %collective-permute-start.3 = (bf16[1,1,64,256]{3,2,1,0:T(8,128)(2,1)S(1)}, bf16[1,1,64,256]{3,2,1,0:T(8,128)(2,1)S(1)}, u32[]{:S(2)}, u32[]{:S(2)}) collective-permute-start(bf16[1,1,64,256]{3,2,1,0:T(8,128)(2,1)S(1)} %get-tuple-element.13), channel_id=1, source_target_pairs={{1,0},{2,1},{3,2},{5,4},{6,5},{7,6},{9,8},{10,9},{11,10},{13,12},{... | collective-permute-start | bytes 98312 | tf_op jit(solution)/shard_map/ppermute | solution.py:15
  29.9 0.7 copy-start.7
Sparse Core Ops, SparseCore 0:
  21.6 71.3 all-reduce.6
  96.5 74.8 all-reduce.4
where the time goes:
time: 181 us; the launch traced here: 180 us
  waiting for transfers between devices  136 us (75%)
  between operations  15 us (8%)
  local copies, waits for them, and re-layouts  11.9 us (7%)
  starting transfers between devices  9.53 us (5%)
  matrix products  6.31 us (3%)
    psum x1, waiting for transfers between devices, shards(): summed = lax.psum(row_share, 'dp')  72.3 us
    unnamed x3, waiting for transfers between devices  61.2 us
    unnamed x25, local copies, waits for them, and re-layouts  7.31 us
    ppermute x2, starting transfers between devices, padded_2(): before = lax.ppermute(last, axis, up)  6.87 us
    dot_general x9, matrix products, shards(): jnp.einsum('bhwc,bhwd->cd', window, cotangent, preferred_element_type=jnp...  3.87 us
  transfers between devices with their start and end apart: 6, of which 3 were waited for; matrix products, arithmetic and copies ran while one was open for 5% of the time, Pallas kernels for 0%

commit v1 on v0

--- a/solution.py
+++ b/solution.py
@@ -49,7 +49,7 @@
     local_terms = jnp.stack(tap_rows)
     groups = lax.axis_size("dp")
     row_share = lax.psum_scatter(local_terms, "rows", scatter_dimension=3, tiled=True)
-    summed = lax.psum(row_share, "dp")
+    summed = jnp.sum(lax.all_gather(row_share, "dp"), axis=0)
     batch_total = images.shape[0] * groups
     return (output_maps, grad_input, summed / float(batch_total))
 

time: 181 us -> 187 us (1.033)
  waiting for transfers between devices: 136 us -> 143 us
  starting transfers between devices: 9.53 us -> 6.63 us
    psum x1 -> x0, waiting for transfers between devices: 72.3 us -> none  [shards(): summed = lax.psum(row_share, 'dp')]
    all_gather x0 -> x1, waiting for transfers between devices: none -> 71.5 us  [shards(): summed = jnp.sum(lax.all_gather(row_share, 'dp'), axis=0)]
    unnamed x3, waiting for transfers between devices: 61.2 us -> 69.4 us
    ppermute x2, starting transfers between devices: 6.87 us -> 3.96 us  [padded_2(): before = lax.ppermute(last, axis, up)]
    reduce_sum x0 -> x1, other arithmetic: none -> 2.72 us  [shards(): summed = jnp.sum(lax.all_gather(row_share, 'dp'), axis=0)]
    unnamed x25 -> x26, local copies, waits for them, and re-layouts: 7.31 us -> 6.71 us
  transfers between devices with their start and end apart: 6 -> 6, of which waited for: 3 -> 3; matrix products, arithmetic and copies ran while one was open for 5% -> 4% of each run, Pallas kernels for 0% -> 0%
where the time goes in v1:
time: 187 us
  waiting for transfers between devices  143 us (76%)
  between operations  15 us (8%)
  local copies, waits for them, and re-layouts  12.2 us (7%)
  starting transfers between devices  6.63 us (4%)
  matrix products  6.31 us (3%)
  other arithmetic  3.18 us (2%)
    all_gather x1, waiting for transfers between devices, shards(): summed = jnp.sum(lax.all_gather(row_share, 'dp'), axis=0)  71.5 us
    unnamed x3, waiting for transfers between devices  69.4 us
    unnamed x26, local copies, waits for them, and re-layouts  6.71 us
    ppermute x2, starting transfers between devices, padded_2(): before = lax.ppermute(last, axis, up)  3.96 us
    dot_general x9, matrix products, shards(): jnp.einsum('bhwc,bhwd->cd', window, cotangent, preferred_element_type=jnp...  3.87 us
  transfers between devices with their start and end apart: 6, of which 3 were waited for; matrix products, arithmetic and copies ran while one was open for 4% of the time, Pallas kernels for 0%

profile of v1, /device:TPU:0, one launch (start us, length us, event | category | flops | bytes accessed | tf_op | source)
XLA Modules:
  0.0 186.7 jit_solution(199234966947611152)
XLA Ops:
  7.2 0.0 copy-start
  7.2 0.0 copy-start.3
  7.2 0.0 copy-start.1
  7.2 0.0 all-reduce.4.cloned.1.call-start
  7.2 0.9 fusion.67
  8.2 2.3 %collective-permute-start = (bf16[1,1,64,256]{3,2,1,0:T(8,128)(2,1)S(1)}, bf16[1,1,64,256]{3,2,1,0:T(8,128)(2,1)S(1)}, u32[]{:S(2)}, u32[]{:S(2)}) collective-permute-start(bf16[1,1,64,256]{3,2,1,0:T(8,128)(2,1)S(1)} %get-tuple-element.12), channel_id=1, source_target_pairs={{0,1},{1,2},{2,3},{4,5},{5,6},{6,7},{8,9},{9,10},{10,11},{12,13},{... | collective-permute-start | bytes 98312 | tf_op jit(solution)/shard_map/ppermute | solution.py:14
  10.5 1.3 collective-permute-start.1
  11.8 1.4 convolution_bitcast_fusion.4
  13.2 0.0 collective-permute-done
  13.3 0.0 copy-done.3
  13.3 2.4 %collective-permute-done.1 = bf16[1,1,64,256]{3,2,1,0:T(8,128)(2,1)S(1)} collective-permute-done((bf16[1,1,64,256]{3,2,1,0:T(8,128)(2,1)S(1)}, bf16[1,1,64,256]{3,2,1,0:T(8,128)(2,1)S(1)}, u32[]{:S(2)}, u32[]{:S(2)}) %collective-permute-start.1) | collective-permute-done | bytes 32800 | tf_op jit(solution)/shard_map/ppermute | solution.py:15
  15.7 0.0 copy-done.1
  15.7 0.0 copy-start.4
  15.7 0.3 convolution_bitcast_fusion.3
  16.0 0.3 convolution_bitcast_fusion.5
  16.4 0.3 convolution_bitcast_fusion.6
  16.7 0.3 convolution_bitcast_fusion.8
  17.0 0.3 convolution_bitcast_fusion
  17.3 0.0 copy-done.4
  17.3 0.3 convolution_bitcast_fusion.2
  17.6 0.3 convolution_bitcast_fusion.1
  17.9 0.1 maximum_bitcast_fusion.2
  18.0 0.3 convolution_bitcast_fusion.7
  18.3 0.1 maximum_bitcast_fusion
  18.4 0.2 pad_maximum_fusion
  18.6 2.9 %copy.24 = f32[3,3,256,256]{2,1,0,3:T(4,128)} copy(f32[3,3,256,256]{3,2,1,0:T(8,128)S(1)} %pad_maximum_fusion) | data formatting | bytes 4718592 | tf_op jit(solution)/shard_map/stack | solution.py:49
  21.5 0.0 copy-start.6
  21.5 0.0 all-reduce.4.cloned.1.call-update
  21.5 0.0 all-gather.3.cloned.1.call-start
  21.6 0.6 copy-done.6
  22.1 0.6 dynamic-slice
  23.4 69.3 %all-reduce.4.cloned.1.call-done = f32[3,3,256,256]{2,1,0,3:T(4,128)} async-done(((f32[3,3,256,256]{2,1,0,3:T(4,128)}), f32[3,3,256,256]{2,1,0,3:T(4,128)}) %all-reduce.4.cloned.1.call-update) | async-done | bytes 2359312
  92.7 1.3 constant_dynamic-slice_fusion
  94.0 0.0 copy-start.2
  94.0 0.0 copy-start.5
  94.0 0.9 copy.25
  94.9 0.0 all-gather.3.cloned.1.call-update
  94.9 0.0 copy-done.2
  95.0 1.6 collective-permute-start.2
  96.6 1.3 collective-permute-start.3
  97.9 0.0 copy-done.5
  97.9 0.3 copy.31
  98.2 0.0 copy-start.7
  98.2 0.1 pad.5.clone
  98.3 0.2 copy.18
  98.5 0.0 copy-done
  98.5 0.4 copy-done.7
  98.9 1.2 fusion
  100.1 0.1 copy.19
  100.2 0.9 copy.27
  101.1 0.0 collective-permute-done.2
  101.1 0.0 collective-permute-done.3
  101.1 0.1 maximum_bitcast_fusion.3
  101.2 0.3 copy.32
  101.4 0.1 pad.7.clone
  101.5 0.2 copy.22
  101.7 1.2 fusion.1
  102.9 0.1 copy.23
  103.1 0.9 copy.28
  104.0 71.5 %all-gather.3.cloned.1.call-done = f32[24,3,256,64]{2,3,1,0:T(8,128)} async-done(((f32[3,3,256,64]{2,3,1,0:T(8,128)}), f32[24,3,256,64]{2,3,1,0:T(8,128)}) %all-gather.3.cloned.1.call-update) | async-done | bytes 4718608 | tf_op jit(solution)/shard_map/all_gather | solution.py:52
  175.5 2.7 %reduce_sum.9 = f32[3,3,256,64]{2,3,1,0:T(8,128)S(1)} reduce(f32[8,3,3,256,64]{3,4,2,1,0:T(8,128)} %bitcast.100, f32[]{:T(128)} %constant.6.clone.1), dimensions={0}, to_apply=%region_1.2 | reduce | flops 1032192 | bytes 5308420 | tf_op jit(solution)/shard_map/reduce_sum | solution.py:52
  178.2 0.4 copy.30
  178.6 0.1 broadcast_multiply_fusion
  178.7 1.2 copy.29
  (8 shorter events, 0.2 us)
Async XLA Ops:
  7.2 91.3 %copy-start = (bf16[3,3,256,256]{3,2,1,0:T(8,128)(2,1)S(1)}, bf16[3,3,256,256]{3,2,1,0:T(8,128)(2,1)}, u32[]{:S(2)}) copy-start(bf16[3,3,256,256]{3,2,1,0:T(8,128)(2,1)} %param.4) | copy-start | bytes 3538948
  7.2 6.1 %copy-start.3 = (bf16[1,12,64,256]{3,2,1,0:T(8,128)(2,1)S(1)}, bf16[1,12,64,256]{3,2,1,0:T(8,128)(2,1)}, u32[]{:S(2)}) copy-start(bf16[1,12,64,256]{3,2,1,0:T(8,128)(2,1)} %param.3) | copy-start | bytes 1179652
  7.2 8.5 %copy-start.1 = (bf16[1,12,64,256]{3,2,1,0:T(8,128)(2,1)S(1)}, bf16[1,12,64,256]{3,2,1,0:T(8,128)(2,1)}, u32[]{:S(2)}) copy-start(bf16[1,12,64,256]{3,2,1,0:T(8,128)(2,1)} %param.5) | copy-start | bytes 1179652
  7.2 85.5 %all-reduce.4.cloned.1.call-start = ((), (), s32[]{:S(2)}) async-start(), calls=%async_computation.1 | async-start | bytes 6291456
  8.2 5.1 %collective-permute-start = (bf16[1,1,64,256]{3,2,1,0:T(8,128)(2,1)S(1)}, bf16[1,1,64,256]{3,2,1,0:T(8,128)(2,1)S(1)}, u32[]{:S(2)}, u32[]{:S(2)}) collective-permute-start(bf16[1,1,64,256]{3,2,1,0:T(8,128)(2,1)S(1)} %get-tuple-element.12), channel_id=1, source_target_pairs={{0,1},{1,2},{2,3},{4,5},{5,6},{6,7},{8,9},{9,10},{10,11},{12,13},{... | collective-permute-start | bytes 98312 | tf_op jit(solution)/shard_map/ppermute | solution.py:14
  10.5 5.2 %collective-permute-start.1 = (bf16[1,1,64,256]{3,2,1,0:T(8,128)(2,1)S(1)}, bf16[1,1,64,256]{3,2,1,0:T(8,128)(2,1)S(1)}, u32[]{:S(2)}, u32[]{:S(2)}) collective-permute-start(bf16[1,1,64,256]{3,2,1,0:T(8,128)(2,1)S(1)} %get-tuple-element.11), channel_id=1, source_target_pairs={{1,0},{2,1},{3,2},{5,4},{6,5},{7,6},{9,8},{10,9},{11,10},{13,12},{... | collective-permute-start | bytes 98312 | tf_op jit(solution)/shard_map/ppermute | solution.py:15
  15.7 1.6 copy-start.4
  21.5 0.7 copy-start.6
  21.5 154.0 %all-gather.3.cloned.1.call-start = ((), (), s32[]{:S(2)}) async-start(), calls=%async_computation | async-start | bytes 5308416 | tf_op jit(solution)/shard_map/all_gather | solution.py:52
  94.0 1.0 copy-start.2
  94.0 3.9 %copy-start.5 = (bf16[1,14,64,256]{3,2,1,0:T(8,128)(2,1)S(1)}, bf16[1,14,64,256]{3,2,1,0:T(8,128)(2,1)}, u32[]{:S(2)}) copy-start(bf16[1,14,64,256]{3,2,1,0:T(8,128)(2,1)} %copy-done.4) | copy-start | bytes 1376260
  95.0 6.1 %collective-permute-start.2 = (bf16[1,1,64,256]{3,2,1,0:T(8,128)(2,1)S(1)}, bf16[1,1,64,256]{3,2,1,0:T(8,128)(2,1)S(1)}, u32[]{:S(2)}, u32[]{:S(2)}) collective-permute-start(bf16[1,1,64,256]{3,2,1,0:T(8,128)(2,1)S(1)} %get-tuple-element.9), channel_id=1, source_target_pairs={{0,1},{1,2},{2,3},{4,5},{5,6},{6,7},{8,9},{9,10},{10,11},{12,13},{... | collective-permute-start | bytes 98312 | tf_op jit(solution)/shard_map/ppermute | solution.py:14
  96.6 4.5 %collective-permute-start.3 = (bf16[1,1,64,256]{3,2,1,0:T(8,128)(2,1)S(1)}, bf16[1,1,64,256]{3,2,1,0:T(8,128)(2,1)S(1)}, u32[]{:S(2)}, u32[]{:S(2)}) collective-permute-start(bf16[1,1,64,256]{3,2,1,0:T(8,128)(2,1)S(1)} %get-tuple-element.10), channel_id=1, source_target_pairs={{1,0},{2,1},{3,2},{5,4},{6,5},{7,6},{9,8},{10,9},{11,10},{13,12},{... | collective-permute-start | bytes 98312 | tf_op jit(solution)/shard_map/ppermute | solution.py:15
  98.2 0.7 copy-start.7
Sparse Core Ops, SparseCore 0:
  21.6 71.0 all-reduce.3
  95.5 79.9 all-gather.2
